TPU v7x, 32 devices: a whole 2x2x4 slice. The times are simulated.
32 devices in a mesh: grp: 2 (over core), pen: 8 (over z, x), gz: 2 (over y).
Axes of the slice: x: 2, y: 2, z: 4, core: 2. Of those that a mesh axis runs over, the one named last changes fastest.
Arguments:
- velocity: float32 [4, 3, 4, 512, 256], P('grp', None, 'gz', 'pen'), may hold values from -6 to 6
- fringe_source: int32 [192], replicated, may hold values from 0 to 255
- blend_index: int32 [192], replicated, may hold values from 0 to 15
- blend_table: float32 [16], replicated, may hold values from 0.2 to 1
Outputs:
- velocity_next: float32 [4, 3, 4, 512, 256], P('grp', None, 'gz', 'pen')
All inputs are finite; a program needn't handle non-finite values.
Results may differ from a plain program's by a relative error of at most 0.0003.
Values sent between devices are 32-bit elements; how exact they have to be, the bound alone decides.
A program may use at most 64 MiB of HBM per device.

v0:
```python
import jax
import jax.numpy as jnp
from jax import lax
from jax.sharding import PartitionSpec as P

NY = 512


SMAGORINSKY = 0.04
TIMESTEP = 0.1
HIGHEST = lax.Precision.HIGHEST


def with_halo(cells, sides, width):
    for axis, dim in sides:
        count = lax.axis_size(axis)
        ends = count - 1
        head = lax.slice_in_dim(cells, 0, width, axis=dim)
        tail = lax.slice_in_dim(cells, cells.shape[dim] - width, cells.shape[dim], axis=dim)
        cells = jnp.concatenate(
            [
                lax.ppermute(tail, axis, [(i, (i + 1) % count) for i in range(ends)]),
                cells,
                lax.ppermute(head, axis, [((i + 1) % count, i) for i in range(ends)]),
            ],
            axis=dim,
        )
    return cells


def passed_along(block, axis, distance):
    devices = range(lax.axis_size(axis))
    route = [(i - distance, i) for i in devices if i - distance in devices]
    return lax.ppermute(block, axis, route)


def cotangent_entries(offset, length):
    half_length = length // 2
    reduced = jnp.remainder(offset + half_length, length) - half_length
    nonzero = reduced != 0
    phase_angle = jnp.pi * reduced.astype(jnp.float32) / length.astype(jnp.float32)
    sine_value = jnp.where(nonzero, jnp.sin(phase_angle), 1.0)
    parity = jnp.remainder(reduced, 2).astype(jnp.float32)
    step_scale = jnp.pi / length.astype(jnp.float32)
    return jnp.where(
        nonzero, (1.0 - 2.0 * parity) * step_scale * jnp.cos(phase_angle) / sine_value, 0.0
    )


def span_table(line_length, groups):
    rows_each = line_length // groups
    order_ids = jnp.arange(line_length, dtype=jnp.int32)
    cell_ids = order_ids % rows_each * groups + order_ids // rows_each
    return cotangent_entries(
        cell_ids[None, :] - cell_ids[:, None], jnp.asarray(line_length, jnp.int32)
    )


def block_operator(out_ids, in_ids, block_width):
    cell_ids = jnp.arange(block_width, dtype=jnp.int32)
    farm_out = out_ids < 3
    farm_in = in_ids < 3
    out_stride = jnp.where(farm_out, 3, 1).astype(jnp.int32)
    in_stride = jnp.where(farm_in, 3, 1).astype(jnp.int32)
    out_cell = (
        jnp.where(farm_out, out_ids, 0)[:, None, None, None]
        + out_stride[:, None, None, None] * cell_ids[None, :, None, None]
    )
    in_cell = (
        jnp.where(farm_in, in_ids, 0)[None, None, :, None]
        + in_stride[None, None, :, None] * cell_ids[None, None, None, :]
    )
    length = jnp.where(farm_out, 3 * block_width, block_width).astype(jnp.int32)[
        :, None, None, None
    ]
    coupled = farm_out[:, None, None, None] == farm_in[None, None, :, None]
    return jnp.where(coupled, cotangent_entries(out_cell - in_cell, length), 0.0)


def strain_terms(col_speed, gradients):
    strain = {}
    squares = jnp.zeros_like(col_speed[:, 0])
    for comp_a in range(3):
        for comp_b in range(comp_a, 3):
            strain_value = 0.5 * (gradients[comp_b][:, comp_a] + gradients[comp_a][:, comp_b])
            strain[comp_a, comp_b] = strain_value
            strain[comp_b, comp_a] = strain_value
            weight_sq = 1.0 if comp_a == comp_b else 2.0
            squares = squares + weight_sq * strain_value * strain_value
    eddy_visc = SMAGORINSKY * jnp.sqrt(2.0 * squares)
    fluxes = [
        jnp.stack([2.0 * eddy_visc * strain[comp_a, comp_b] for comp_a in range(3)], axis=1)
        for comp_b in range(3)
    ]
    advect = sum((col_speed[:, comp_b : comp_b + 1] * gradients[comp_b] for comp_b in range(3)))
    return (fluxes, advect)


def vertical_difference(padded):
    return 0.5 * (padded[:, :, 2:] - padded[:, :, :-2])


def per_device(velocity, fringe_source, blend_index, blend_table):
    group_id = lax.axis_index("grp")
    blocks_here = velocity.shape[0]
    block_width = velocity.shape[-1]
    local_ids = blocks_here * group_id + jnp.arange(blocks_here, dtype=jnp.int32)
    spanwise = span_table(NY, lax.axis_size("pen"))

    def add_stream_terms(shards):
        in_ids = jnp.arange(shards.shape[0], dtype=jnp.int32)
        operator = block_operator(local_ids, in_ids, block_width)
        return jnp.einsum("mczyl,jiml->jczyi", shards, operator, precision=HIGHEST)

    def span_derivative(columns):
        return jnp.einsum("bczyx,yk->bczkx", columns, spanwise, precision=HIGHEST)

    grad_x = add_stream_terms(lax.all_gather(velocity, "grp", axis=0, tiled=True))
    grad_z = vertical_difference(with_halo(velocity, (("gz", 2),), 1))
    columns = lax.all_to_all(velocity, "pen", split_axis=4, concat_axis=3, tiled=True)
    grad_y = lax.all_to_all(
        span_derivative(columns), "pen", split_axis=3, concat_axis=4, tiled=True
    )
    fluxes, advect = strain_terms(velocity, (grad_x, grad_y, grad_z))
    flux_columns = lax.all_to_all(fluxes[1], "pen", split_axis=4, concat_axis=3, tiled=True)
    flux_y = lax.all_to_all(
        span_derivative(flux_columns), "pen", split_axis=3, concat_axis=4, tiled=True
    )
    flux_z = vertical_difference(with_halo(fluxes[2], (("gz", 2),), 1))
    partial_sum = flux_y + flux_z - advect
    flux_x = fluxes[0]
    stream_div = add_stream_terms(lax.all_gather(flux_x, "grp", axis=0, tiled=True))
    stepped = velocity + TIMESTEP * (partial_sum + stream_div)
    table_ids = jnp.arange(blend_table.shape[0], dtype=jnp.int32)
    weights = jnp.sum(
        blend_table[None, :] * (blend_index[:, None] == table_ids[None, :]).astype(jnp.float32),
        axis=1,
    )
    fringe_third = fringe_source.shape[0] // 3
    source_by_block = fringe_source.reshape(fringe_third, 3).T
    weight_by_block = weights.reshape(fringe_third, 3).T
    slot_block = jnp.minimum(local_ids, 2)
    slot_farm = local_ids < 3
    slot_source = source_by_block[slot_block]
    slot_weight = jnp.where(slot_farm[:, None], weight_by_block[slot_block], 0.0)
    whole_block = passed_along(stepped[1], "grp", -1)
    inflow_here = jnp.where(group_id == 0, whole_block, stepped[1])
    sources = [jnp.take(inflow_here, slot_source[slot], axis=-1) for slot in range(2)]
    pieces = []
    for slot in range(2):
        fringe_head = stepped[slot, ..., :fringe_third]
        mixed_head = fringe_head + slot_weight[slot] * (sources[slot] - fringe_head)
        pieces.append(jnp.concatenate([mixed_head, stepped[slot, ..., fringe_third:]], axis=-1))
    return jnp.stack(pieces)


def solution(mesh):
    placed = (P("grp", None, "gz", "pen", None), P(), P(), P())
    return jax.shard_map(
        per_device,
        mesh=mesh,
        in_specs=placed,
        out_specs=P("grp", None, "gz", "pen", None),
        check_vma=False,
    )
```

profile of v0, /device:TPU:0, one launch (start us, length us, event | category | flops | bytes accessed | tf_op | source)
XLA Modules:
  0.0 258.0 jit_solution(6300955613318501670)
XLA Ops:
  12.3 7.3 %all-to-all-start = ((f32[8,1,24576]{2,1,0:T(1,128)}), f32[8,1,24576]{2,1,0:T(1,128)S(1)}, u32[]{:S(2)}, u32[]{:S(2)}) async-start(f32[8,1,24576]{2,1,0:T(1,128)} %reshape.312), calls=%async_computation | async-start | bytes 1572864 | tf_op jit(solution)/shard_map/all_to_all | solution.py:120
  21.8 5.8 %collective-permute-start.1 = (f32[2,3,1,64,256]{4,3,2,1,0:T(8,128)}, f32[2,3,1,64,256]{4,3,2,1,0:T(8,128)}, u32[]{:S(2)}, u32[]{:S(2)}) collective-permute-start(f32[2,3,1,64,256]{4,3,2,1,0:T(8,128)} %get-tuple-element.28), channel_id=1, source_target_pairs={{0,1},{2,3},{4,5},{6,7},{8,9},{10,11},{12,13},{14,15},{16,17},{18,... | collective-permute-start | bytes 1179656 | tf_op jit(solution)/shard_map/ppermute | solution.py:22
  30.6 9.2 %all-to-all-done = f32[8,1,24576]{2,1,0:T(1,128)S(1)} async-done(((f32[8,1,24576]{2,1,0:T(1,128)}), f32[8,1,24576]{2,1,0:T(1,128)S(1)}, u32[]{:S(2)}, u32[]{:S(2)}) %all-to-all-start) | async-done | bytes 786464 | tf_op jit(solution)/shard_map/all_to_all | solution.py:120
  45.6 6.7 %convolution_bitcast_fusion.1 = f32[2,3,2,512,32]{3,4,2,1,0:T(8,128)S(1)} fusion(f32[2,3,2,512,32]{3,4,2,1,0:T(8,128)S(1)} %all_to_all.55, s32[512]{0:T(512)S(1)} %fusion.90), kind=kOutput, calls=%fused_computation.39 | convolution fusion | flops 1217396736 | bytes 1574912 | tf_op jit(solution)/shard_map/bczyx,yk->bczkx/dot_general | solution.py:116
  52.3 3.5 %copy.57 = f32[2,3,2,512,32]{4,2,1,0,3:T(2,128)} copy(f32[2,3,2,512,32]{3,4,2,1,0:T(8,128)S(1)} %convolution_bitcast_fusion.1) | data formatting | bytes 1572864 | tf_op jit(solution)/shard_map/bczyx,yk->bczkx/transpose | solution.py:116
  55.8 5.3 %reshape.314 = f32[8,1,24576]{2,1,0:T(1,128)} reshape(f32[512,2,3,2,32]{4,3,2,1,0:T(2,128)} %bitcast.148) | data formatting | bytes 1572864
  61.0 3.6 %all-to-all-start.1 = ((f32[8,1,24576]{2,1,0:T(1,128)}), f32[8,1,24576]{2,1,0:T(1,128)S(1)}, u32[]{:S(2)}, u32[]{:S(2)}) async-start(f32[8,1,24576]{2,1,0:T(1,128)} %reshape.314), calls=%async_computation.1 | async-start | bytes 1572864 | tf_op jit(solution)/shard_map/all_to_all | solution.py:121
  66.9 34.7 %fusion.21 = f32[2,3,2,64,256]{4,3,2,1,0:T(8,128)} fusion(f32[4,3,2,64,256]{4,3,0,2,1:T(8,128)} %all-gather.3.cloned.1.call-done, s32[2]{0:T(128)S(1)} %fusion.96, f32[2]{0:T(128)S(1)} %copy-done.14, f32[2]{0:T(128)S(1)} %copy-done.18, s32[2]{0:T(128)S(1)} %copy-done.12, s32[4,256]{1,0:T(4,128)S(1)} %multiply_add_fusion, ...), kind=kOutput, calls=%fused_computation.36 | convolution fusion | flops 2433220608 | bytes 2365480 | tf_op jit(solution)/shard_map/mczyl,jiml->jczyi/dot_general | solution.py:113
  104.1 4.3 %reshape.315 = f32[512,2,3,2,32]{4,3,2,1,0:T(2,128)} reshape(f32[8,24576]{1,0:T(8,128)S(1)} %reduce.1) | data formatting | bytes 1572864
  108.4 4.0 %copy.58 = f32[2,3,2,8,64,32]{4,5,3,2,1,0:T(8,128)S(1)} copy(f32[2,3,2,8,64,32]{5,2,1,0,4,3:T(2,128)} %bitcast.146) | data formatting | bytes 1572864 | tf_op jit(solution)/shard_map/all_to_all | solution.py:121
  116.4 2.6 copy.62
  118.9 2.5 reshape.316
  121.5 6.0 %all-to-all-start.2 = ((f32[8,1,24576]{2,1,0:T(1,128)}), f32[8,1,24576]{2,1,0:T(1,128)S(1)}, u32[]{:S(2)}, u32[]{:S(2)}) async-start(f32[8,1,24576]{2,1,0:T(1,128)} %reshape.316), calls=%async_computation.2 | async-start | bytes 1572864 | tf_op jit(solution)/shard_map/all_to_all | solution.py:125
  128.2 19.1 %all-to-all-done.2 = f32[8,1,24576]{2,1,0:T(1,128)S(1)} async-done(((f32[8,1,24576]{2,1,0:T(1,128)}), f32[8,1,24576]{2,1,0:T(1,128)S(1)}, u32[]{:S(2)}, u32[]{:S(2)}) %all-to-all-start.2) | async-done | bytes 786464 | tf_op jit(solution)/shard_map/all_to_all | solution.py:125
  147.3 3.7 %reduce.2 = f32[8,24576]{1,0:T(8,128)} reduce(f32[8,1,24576]{2,1,0:T(1,128)S(1)} %all-to-all-done.2, f32[]{:T(128)} %broadcast.662), dimensions={1}, to_apply=%all_to_all.60.reduce_sub_computation | reduce | bytes 1572868 | tf_op jit(solution)/shard_map/all_to_all | solution.py:125
  155.8 7.8 %convolution_bitcast_fusion = f32[2,3,2,512,32]{3,4,2,1,0:T(8,128)S(1)} fusion(f32[2,3,2,512,32]{3,4,2,1,0:T(8,128)} %all_to_all.63, s32[512]{0:T(512)S(1)} %fusion.90), kind=kOutput, calls=%fused_computation.38 | convolution fusion | flops 1217396736 | bytes 1574912 | tf_op jit(solution)/shard_map/bczyx,yk->bczkx/dot_general | solution.py:116
  163.6 3.9 %copy.65 = f32[2,3,2,512,32]{4,2,1,0,3:T(2,128)} copy(f32[2,3,2,512,32]{3,4,2,1,0:T(8,128)S(1)} %convolution_bitcast_fusion) | data formatting | bytes 1572864 | tf_op jit(solution)/shard_map/bczyx,yk->bczkx/transpose | solution.py:116
  167.5 5.3 %reshape.318 = f32[8,1,24576]{2,1,0:T(1,128)} reshape(f32[512,2,3,2,32]{4,3,2,1,0:T(2,128)} %bitcast.149) | data formatting | bytes 1572864
  172.8 3.5 %all-to-all-start.3 = ((f32[8,1,24576]{2,1,0:T(1,128)}), f32[8,1,24576]{2,1,0:T(1,128)S(1)}, u32[]{:S(2)}, u32[]{:S(2)}) async-start(f32[8,1,24576]{2,1,0:T(1,128)} %reshape.318), calls=%async_computation.3 | async-start | bytes 1572864 | tf_op jit(solution)/shard_map/all_to_all | solution.py:126
  180.4 6.1 %collective-permute-start.3 = (f32[2,3,1,64,256]{4,3,2,1,0:T(8,128)}, f32[2,3,1,64,256]{4,3,2,1,0:T(8,128)}, u32[]{:S(2)}, u32[]{:S(2)}) collective-permute-start(f32[2,3,1,64,256]{4,3,2,1,0:T(8,128)} %get-tuple-element.26), channel_id=1, source_target_pairs={{0,1},{2,3},{4,5},{6,7},{8,9},{10,11},{12,13},{14,15},{16,17},{18,... | collective-permute-start | bytes 1179656 | tf_op jit(solution)/shard_map/ppermute | solution.py:22
  187.5 9.2 %all-to-all-done.3 = f32[8,1,24576]{2,1,0:T(1,128)S(1)} async-done(((f32[8,1,24576]{2,1,0:T(1,128)}), f32[8,1,24576]{2,1,0:T(1,128)S(1)}, u32[]{:S(2)}, u32[]{:S(2)}) %all-to-all-start.3) | async-done | bytes 786464 | tf_op jit(solution)/shard_map/all_to_all | solution.py:126
  199.2 4.3 %reshape.319 = f32[512,2,3,2,32]{4,3,2,1,0:T(2,128)} reshape(f32[8,24576]{1,0:T(8,128)S(1)} %reduce.3) | data formatting | bytes 1572864
  203.5 4.0 %copy.66 = f32[2,3,2,8,64,32]{4,5,3,2,1,0:T(8,128)S(1)} copy(f32[2,3,2,8,64,32]{5,2,1,0,4,3:T(2,128)} %bitcast.147) | data formatting | bytes 1572864 | tf_op jit(solution)/shard_map/all_to_all | solution.py:126
  208.9 34.6 %fusion.41 = f32[2,3,2,64,256]{4,3,2,1,0:T(8,128)S(1)} fusion(f32[2,3,2,64,256]{4,3,2,1,0:T(8,128)S(1)} %copy-done, f32[4,3,2,64,256]{4,3,2,1,0:T(8,128)} %all-gather.5.cloned.1.call-done, s32[2]{0:T(128)S(1)} %copy-done.21, f32[2]{0:T(128)S(1)} %copy-done.15, f32[2]{0:T(128)S(1)} %copy-done.19, s32[2]{0:T(128)S(1)} %copy-done.13, ...), kind=kOutput, calls=%fused_computation.42 | convolution fusion | flops 2437349376 | bytes 8656936 | tf_op jit(solution)/shard_map/mczyl,jiml->jczyi/dot_general | solution.py:113
  (119 shorter events, 47.2 us)
Async XLA Ops:
  6.5 2.2 copy-start
  6.5 60.3 %all-gather.3.cloned.1.call-start = ((), (), s32[]{:S(2)}) async-start(), calls=%async_computation.4 | async-start | bytes 2359296 | tf_op jit(solution)/shard_map/all_gather | solution.py:118
  12.3 27.4 %all-to-all-start = ((f32[8,1,24576]{2,1,0:T(1,128)}), f32[8,1,24576]{2,1,0:T(1,128)S(1)}, u32[]{:S(2)}, u32[]{:S(2)}) async-start(f32[8,1,24576]{2,1,0:T(1,128)} %reshape.312), calls=%async_computation | async-start | bytes 1572864 | tf_op jit(solution)/shard_map/all_to_all | solution.py:120
  20.5 44.2 %collective-permute-start = (f32[2,3,1,64,256]{4,3,2,1,0:T(8,128)}, f32[2,3,1,64,256]{4,3,2,1,0:T(8,128)S(1)}, u32[]{:S(2)}, u32[]{:S(2)}) collective-permute-start(f32[2,3,1,64,256]{4,3,2,1,0:T(8,128)} %get-tuple-element.27), channel_id=1, source_target_pairs={{1,0},{3,2},{5,4},{7,6},{9,8},{11,10},{13,12},{15,14},{17,16},{19,... | collective-permute-start | bytes 1179656 | tf_op jit(solution)/shard_map/ppermute | solution.py:24
  21.8 42.9 %collective-permute-start.1 = (f32[2,3,1,64,256]{4,3,2,1,0:T(8,128)}, f32[2,3,1,64,256]{4,3,2,1,0:T(8,128)}, u32[]{:S(2)}, u32[]{:S(2)}) collective-permute-start(f32[2,3,1,64,256]{4,3,2,1,0:T(8,128)} %get-tuple-element.28), channel_id=1, source_target_pairs={{0,1},{2,3},{4,5},{6,7},{8,9},{10,11},{12,13},{14,15},{16,17},{18,... | collective-permute-start | bytes 1179656 | tf_op jit(solution)/shard_map/ppermute | solution.py:22
  55.7 8.9 %copy-start.10 = (s32[4]{0:T(128)S(1)}, s32[4]{0:T(128)}, u32[]{:S(2)}) copy-start(s32[4]{0:T(128)} %get-tuple-element.40) | copy-start | bytes 52
  55.7 8.9 %copy-start.11 = (s32[4]{0:T(128)S(1)}, s32[4]{0:T(128)}, u32[]{:S(2)}) copy-start(s32[4]{0:T(128)} %get-tuple-element.41) | copy-start | bytes 52
  61.0 5.8 %copy-start.12 = (s32[2]{0:T(128)S(1)}, s32[2]{0:T(128)}, u32[]{:S(2)}) copy-start(s32[2]{0:T(128)} %get-tuple-element.36) | copy-start | bytes 28
  61.0 5.8 %copy-start.14 = (f32[2]{0:T(128)S(1)}, f32[2]{0:T(128)}, u32[]{:S(2)}) copy-start(f32[2]{0:T(128)} %get-tuple-element.38) | copy-start | bytes 28
  61.0 5.8 %copy-start.16 = (pred[2,4]{1,0:T(4,128)(4,1)S(1)}, pred[2,4]{1,0:T(4,128)(4,1)}, u32[]{:S(2)}) copy-start(pred[2,4]{1,0:T(4,128)(4,1)} %broadcast_compare_fusion) | copy-start | bytes 28
  61.0 5.8 %copy-start.18 = (f32[2]{0:T(128)S(1)}, f32[2]{0:T(128)}, u32[]{:S(2)}) copy-start(f32[2]{0:T(128)} %broadcast_divide_fusion) | copy-start | bytes 28
  61.0 40.5 %all-to-all-start.1 = ((f32[8,1,24576]{2,1,0:T(1,128)}), f32[8,1,24576]{2,1,0:T(1,128)S(1)}, u32[]{:S(2)}, u32[]{:S(2)}) async-start(f32[8,1,24576]{2,1,0:T(1,128)} %reshape.314), calls=%async_computation.1 | async-start | bytes 1572864 | tf_op jit(solution)/shard_map/all_to_all | solution.py:121
  64.6 36.9 %copy-start.20 = (s32[2]{0:T(128)}, s32[2]{0:T(128)S(1)}, u32[]{:S(2)}) copy-start(s32[2]{0:T(128)S(1)} %fusion.96) | copy-start | bytes 28
  64.7 36.8 %copy-start.6 = (f32[2,3,1,64,256]{4,3,2,1,0:T(8,128)}, f32[2,3,1,64,256]{4,3,2,1,0:T(8,128)S(1)}, u32[]{:S(2)}) copy-start(f32[2,3,1,64,256]{4,3,2,1,0:T(8,128)S(1)} %collective-permute-done) | copy-start | bytes 1179652
  121.5 25.9 %all-to-all-start.2 = ((f32[8,1,24576]{2,1,0:T(1,128)}), f32[8,1,24576]{2,1,0:T(1,128)S(1)}, u32[]{:S(2)}, u32[]{:S(2)}) async-start(f32[8,1,24576]{2,1,0:T(1,128)} %reshape.316), calls=%async_computation.2 | async-start | bytes 1572864 | tf_op jit(solution)/shard_map/all_to_all | solution.py:125
  127.5 81.4 %all-gather.5.cloned.1.call-start = ((), (), s32[]{:S(2)}) async-start(), calls=%async_computation.5 | async-start | bytes 2359296 | tf_op jit(solution)/shard_map/all_gather | solution.py:132
  167.5 8.9 %copy-start.7 = (s32[192]{0:T(256)S(1)}, s32[192]{0:T(256)}, u32[]{:S(2)}) copy-start(s32[192]{0:T(256)} %param.9) | copy-start | bytes 2308
  167.5 9.1 %copy-start.8 = (s32[192]{0:T(256)S(1)}, s32[192]{0:T(256)}, u32[]{:S(2)}) copy-start(s32[192]{0:T(256)} %param.10) | copy-start | bytes 2308
  167.5 9.1 %copy-start.9 = (f32[16]{0:T(128)S(1)}, f32[16]{0:T(128)}, u32[]{:S(2)}) copy-start(f32[16]{0:T(128)} %param.11) | copy-start | bytes 196
  167.5 10.6 %copy-start.3 = (f32[2,3,2,64,256]{4,3,2,1,0:T(8,128)S(1)}, f32[2,3,2,64,256]{4,3,2,1,0:T(8,128)}, u32[]{:S(2)}) copy-start(f32[2,3,2,64,256]{4,3,2,1,0:T(8,128)} %get-tuple-element.29) | copy-start | bytes 2359300
  172.8 23.9 %all-to-all-start.3 = ((f32[8,1,24576]{2,1,0:T(1,128)}), f32[8,1,24576]{2,1,0:T(1,128)S(1)}, u32[]{:S(2)}, u32[]{:S(2)}) async-start(f32[8,1,24576]{2,1,0:T(1,128)} %reshape.318), calls=%async_computation.3 | async-start | bytes 1572864 | tf_op jit(solution)/shard_map/all_to_all | solution.py:126
  179.1 29.8 %collective-permute-start.2 = (f32[2,3,1,64,256]{4,3,2,1,0:T(8,128)}, f32[2,3,1,64,256]{4,3,2,1,0:T(8,128)}, u32[]{:S(2)}, u32[]{:S(2)}) collective-permute-start(f32[2,3,1,64,256]{4,3,2,1,0:T(8,128)} %get-tuple-element.25), channel_id=1, source_target_pairs={{1,0},{3,2},{5,4},{7,6},{9,8},{11,10},{13,12},{15,14},{17,16},{19,... | collective-permute-start | bytes 1179656 | tf_op jit(solution)/shard_map/ppermute | solution.py:24
  180.4 28.5 %collective-permute-start.3 = (f32[2,3,1,64,256]{4,3,2,1,0:T(8,128)}, f32[2,3,1,64,256]{4,3,2,1,0:T(8,128)}, u32[]{:S(2)}, u32[]{:S(2)}) collective-permute-start(f32[2,3,1,64,256]{4,3,2,1,0:T(8,128)} %get-tuple-element.26), channel_id=1, source_target_pairs={{0,1},{2,3},{4,5},{6,7},{8,9},{10,11},{12,13},{14,15},{16,17},{18,... | collective-permute-start | bytes 1179656 | tf_op jit(solution)/shard_map/ppermute | solution.py:22
  243.5 3.6 %collective-permute-start.4 = (f32[3,2,64,256]{3,2,1,0:T(8,128)S(1)}, f32[3,2,64,256]{3,2,1,0:T(8,128)S(1)}, u32[]{:S(2)}, u32[]{:S(2)}) collective-permute-start(f32[3,2,64,256]{3,2,1,0:T(8,128)S(1)} %slice_bitcast_fusion.2), channel_id=1, source_target_pairs={{16,0},{17,1},{18,2},{19,3},{20,4},{21,5},{22,6},{23,7},{24,8},{25... | collective-permute-start | bytes 1179656 | tf_op jit(solution)/shard_map/ppermute | solution.py:34
  (9 other events, 14.0 us)
Sparse Core Ops, SparseCore 0:
  8.9 12.4 all-gather.2
  129.9 11.2 all-gather.4
where the time goes:
time: 261 us; the launch traced here: 258 us
  matrix products  83.8 us (32%)
  local copies, waits for them, and re-layouts  61.4 us (24%)
  waiting for transfers between devices  40.1 us (15%)
  starting transfers between devices  36.3 us (14%)
  other arithmetic  22.3 us (9%)
  between operations  14.2 us (5%)
    dot_general x2, matrix products, add_stream_terms(): return jnp.einsum('mczyl,jiml->jczyi', shards, operator, precision=HIGHEST)  69.3 us
    unnamed x54, local copies, waits for them, and re-layouts  31 us
    all_to_all x1, waiting for transfers between devices, per_device(): lax.all_to_all(fluxes[1], 'pen', split_axis=4, concat_axis=3, tiled=True)  19.1 us
    dot_general x2, matrix products, span_derivative(): return jnp.einsum('bczyx,yk->bczkx', columns, spanwise, precision=HIGHEST)  14.5 us
    ppermute x2, starting transfers between devices, with_halo(): lax.ppermute(tail, axis, [(i, (i + 1) % count) for i in range(ends)])  11.9 us
    all_to_all x1, waiting for transfers between devices, per_device(): lax.all_to_all(span_derivative(flux_columns), 'pen', split_axis=3, concat...  9.23 us
    all_to_all x1, waiting for transfers between devices, per_device(): lax.all_to_all(velocity, 'pen', split_axis=4, concat_axis=3, tiled=True)  9.15 us
    transpose x2, local copies, waits for them, and re-layouts, span_derivative(): return jnp.einsum('bczyx,yk->bczkx', columns, spanwise, precision=HIGHEST)  7.31 us
  transfers between devices with their start and end apart: 11, of which 4 were waited for; matrix products, arithmetic and copies ran while one was open for 41% of the time, Pallas kernels for 0%

commit v1 on v0

v1 whole, which is shorter than its diff:
```python
import functools

import jax
import jax.numpy as jnp
import ml_dtypes
import numpy as np
from jax import lax
from jax.experimental import pallas as pl
from jax.experimental.pallas import tpu as pltpu
from jax.sharding import PartitionSpec as P

SMAGORINSKY = 0.04
TIMESTEP = 0.1
LANES = 128
SLAB = 16
MESH = pl.DeviceIdType.MESH
F32 = jnp.float32
BF16 = jnp.bfloat16


def cotangent_entries(offset, length):
    half = length // 2
    reduced = (offset + half) % length - half
    angle = np.pi * reduced / length
    safe = np.where(reduced != 0, np.sin(angle), 1.0)
    sign = 1.0 - 2.0 * (reduced % 2)
    return np.where(reduced != 0, sign * (np.pi / length) * np.cos(angle) / safe, 0.0)


def span_table(line_length, groups):
    rows_each = line_length // groups
    order = np.arange(line_length)
    cell = order % rows_each * groups + order // rows_each
    return cotangent_entries(cell[:, None] - cell[None, :], line_length)


def stream_table(width):
    cells = np.arange(width)
    tables = []
    for group in range(2):
        outs = (2 * group, 2 * group + 1)
        ins = outs + (2 - 2 * group, 3 - 2 * group)
        rows = []
        for i in ins:
            row = []
            for o in outs:
                if i < 3 and o < 3:
                    offset = (o + 3 * cells)[None, :] - (i + 3 * cells)[:, None]
                    row.append(cotangent_entries(offset, 3 * width))
                elif i == o:
                    row.append(cotangent_entries(cells[None, :] - cells[:, None], width))
                else:
                    row.append(np.zeros((width, width)))
            rows.append(np.concatenate(row, axis=1))
        tables.append(np.concatenate(rows, axis=0))
    return np.stack(tables)


def two_parts(table):
    high = table.astype(np.float32).astype(ml_dtypes.bfloat16)
    low = (table - high.astype(np.float64)).astype(np.float32).astype(ml_dtypes.bfloat16)
    return np.stack([high, low])


def split(x):
    high = x.astype(BF16)
    return high, (x - high.astype(F32)).astype(BF16)


def dot(a, b):
    return jnp.dot(a, b, preferred_element_type=F32)


def kernel(
    pens, heights, u, source, index, table, wx_hbm, wy_hbm, out,
    wx, wy, upad, urecv, gx, gy, fx, fy, fz, frecv, acc, dy, colu, coly, colf, cold,
    hi, lo, inflow, send, recv, esend, erecv, hsend, hrecv, isend, irecv, lsem,
):
    g = lax.axis_index("grp")
    me = lax.axis_index("pen")
    s = lax.axis_index("gz")
    _, _, levels, rows, width = u.shape
    halves = width // LANES
    chunks = 2 * 3 * levels * halves // pens
    group_count = 2 * levels * halves
    other = 1 - g
    below, above = s > 0, s < heights - 1

    wx_copy = pltpu.make_async_copy(wx_hbm.at[:, g], wx, lsem.at[0])
    wy_copy = pltpu.make_async_copy(wy_hbm, wy, lsem.at[1])
    u_copy = pltpu.make_async_copy(u, upad.at[:, :, pl.ds(1, levels)], lsem.at[2])
    wy_copy.start()
    wx_copy.start()
    u_copy.start()

    barrier = pltpu.get_barrier_semaphore()

    @pl.loop(1, pens)
    def _(i):
        pl.semaphore_signal(
            barrier, inc=1, device_id={"pen": lax.rem(me + i, pens)}, device_id_type=MESH
        )

    pl.semaphore_signal(barrier, inc=1, device_id={"grp": other}, device_id_type=MESH)

    @pl.when(below)
    def _():
        pl.semaphore_signal(barrier, inc=1, device_id={"gz": s - 1}, device_id_type=MESH)

    @pl.when(above)
    def _():
        pl.semaphore_signal(barrier, inc=1, device_id={"gz": s + 1}, device_id_type=MESH)

    levels_near = below.astype(jnp.int32) + above.astype(jnp.int32)
    pl.semaphore_wait(barrier, pens + levels_near)

    def place(group):
        b = 1 - lax.div(group, levels * halves)
        z = lax.rem(lax.div(group, halves), levels)
        return b, z, pl.ds(pl.multiple_of(lax.rem(group, halves) * LANES, LANES), LANES)

    def unit(k, q):
        t = k * pens + q
        b, z, x = place(lax.div(t, 3))
        return b, lax.rem(t, 3), z, slice(None), x

    def band(q):
        return pl.ds(pl.multiple_of(q * rows, rows), rows)

    def pen_copy(src, dst, phase, k, i, q):
        return pltpu.make_async_remote_copy(
            src_ref=src, dst_ref=dst, send_sem=send.at[phase, k, i],
            recv_sem=recv.at[phase, k, i], device_id={"pen": q}, device_id_type=MESH,
        )

    def own_copy(src, dst, phase, k):
        return pltpu.make_async_copy(src, dst, send.at[phase, k, 0])

    def to_lines(field, lines, phase, k):
        own_copy(field.at[unit(k, me)], lines.at[k, band(me)], phase, k).start()

        @pl.loop(1, pens)
        def _(i):
            q = lax.rem(me + i, pens)
            pen_copy(field.at[unit(k, q)], lines.at[k, band(me)], phase, k, i, q).start()

    def lines_here(field, lines, phase, k):
        own_copy(field.at[unit(k, me)], lines.at[k, band(me)], phase, k).wait()

        @pl.loop(1, pens)
        def _(i):
            q = lax.rem(me + pens - i, pens)
            pen_copy(field.at[unit(k, q)], lines.at[k, band(q)], phase, k, i, q).wait_recv()

    def to_rows(lines, field, phase, k):
        own_copy(lines.at[k, band(me)], field.at[unit(k, me)], phase, k).start()

        @pl.loop(1, pens)
        def _(i):
            q = lax.rem(me + i, pens)
            pen_copy(lines.at[k, band(q)], field.at[unit(k, me)], phase, k, i, q).start()

    def rows_here(lines, field, phase, k):
        own_copy(lines.at[k, band(me)], field.at[unit(k, me)], phase, k).wait()

        @pl.loop(1, pens)
        def _(i):
            q = lax.rem(me + pens - i, pens)
            pen_copy(lines.at[k, band(q)], field.at[unit(k, q)], phase, k, i, q).wait_recv()

    def sent(src, dst, phase):
        for k in range(chunks):

            @pl.loop(1, pens)
            def _(i, k=k):
                pen_copy(src, dst, phase, k, i, lax.rem(me + i, pens)).wait_send()

    def span(lines, result, k):
        high, low = split(lines[k])
        both = dot(wy[0], jnp.concatenate([high, low], axis=1))
        result[k] = both[:, :LANES] + both[:, LANES:] + dot(wy[1], high)

    def exchange(src, dst, n):
        return pltpu.make_async_remote_copy(
            src_ref=src, dst_ref=dst, send_sem=esend.at[n], recv_sem=erecv.at[n],
            device_id={"grp": other}, device_id_type=MESH,
        )

    def stream(mine, theirs):
        for b in range(2):
            for at, field in ((b, mine), (b + 2, theirs)):
                high, low = split(field[b].reshape(3 * levels * rows, width))
                hi[:, at * width : (at + 1) * width] = high
                lo[:, at * width : (at + 1) * width] = low

    def stream_out(b):
        cols = slice(b * width, (b + 1) * width)
        part = dot(hi[...], wx[0, :, cols]) + dot(hi[...], wx[1, :, cols])
        part = part + dot(lo[...], wx[0, :, cols])
        return part.reshape(3, levels, rows, width)

    def up_copy(field, n):
        return pltpu.make_async_remote_copy(
            src_ref=field.at[:, :, levels], dst_ref=field.at[:, :, 0],
            send_sem=hsend.at[n, 0], recv_sem=hrecv.at[n, 0],
            device_id={"gz": s + 1}, device_id_type=MESH,
        )

    def down_copy(field, n):
        return pltpu.make_async_remote_copy(
            src_ref=field.at[:, :, 1], dst_ref=field.at[:, :, levels + 1],
            send_sem=hsend.at[n, 1], recv_sem=hrecv.at[n, 1],
            device_id={"gz": s - 1}, device_id_type=MESH,
        )

    def send_levels(field, n):
        @pl.when(above)
        def _():
            up_copy(field, n).start()

        @pl.when(below)
        def _():
            down_copy(field, n).start()

    def levels_here(field, n):
        edge = jnp.zeros((2, 3, rows, width), F32)

        @pl.when(below)
        def _():
            down_copy(field, n).wait_send()
            up_copy(field, n).wait_recv()

        @pl.when(jnp.logical_not(below))
        def _():
            field[:, :, 0] = edge

        @pl.when(above)
        def _():
            up_copy(field, n).wait_send()
            down_copy(field, n).wait_recv()

        @pl.when(jnp.logical_not(above))
        def _():
            field[:, :, levels + 1] = edge

    def over_slabs(first, last, step):
        @pl.loop(first * (rows // SLAB), last * (rows // SLAB))
        def _(n):
            b, z, x = place(lax.div(n, rows // SLAB))
            r = pl.ds(pl.multiple_of(lax.rem(n, rows // SLAB) * SLAB, SLAB), SLAB)
            step(b, z, r, x)

    def fluxes(b, z, r, x):
        speed = [u[b, c, z, r, x] for c in range(3)]
        grad = [
            [gx[b, c, z, r, x] for c in range(3)],
            [gy[b, c, z, r, x] for c in range(3)],
            [0.5 * (upad[b, c, z + 2, r, x] - upad[b, c, z, r, x]) for c in range(3)],
        ]
        for c in range(3):
            acc[b, c, z, r, x] = -(
                speed[0] * grad[0][c] + speed[1] * grad[1][c] + speed[2] * grad[2][c]
            )
        strain = {}
        squares = 0.0
        for i in range(3):
            for j in range(i, 3):
                value = grad[i][i] if i == j else 0.5 * (grad[i][j] + grad[j][i])
                strain[i, j] = strain[j, i] = value
                squares = squares + (1.0 if i == j else 2.0) * value * value
        eddy = (2.0 * SMAGORINSKY) * jnp.sqrt(2.0 * squares)
        for c in range(3):
            fx[b, c, z, r, x] = eddy * strain[c, 0]
            fy[b, c, z, r, x] = eddy * strain[c, 1]
            fz[b, c, z + 1, r, x] = eddy * strain[c, 2]

    def add_rest(b, z, r, x):
        for c in range(3):
            rise = 0.5 * (fz[b, c, z + 2, r, x] - fz[b, c, z, r, x])
            total = acc[b, c, z, r, x] + gx[b, c, z, r, x] + rise
            acc[b, c, z, r, x] = u[b, c, z, r, x] + TIMESTEP * total

    def add_span(b, z, r, x):
        for c in range(3):
            out[b, c, z, r, x] = acc[b, c, z, r, x] + TIMESTEP * dy[b, c, z, r, x]

    def groups_ready(k):
        return (k + 1) * pens // 3

    def groups_needed(k):
        return -(-((k + 1) * pens) // 3)

    x_exchange = exchange(u, urecv, 0)
    x_exchange.start()
    u_copy.wait()
    for k in range(chunks):
        to_lines(u, colu, 0, k)
        if k == 0:
            send_levels(upad, 0)
    wy_copy.wait()
    lines_here(u, colu, 0, 0)
    span(colu, coly, 0)
    to_rows(coly, gy, 1, 0)
    wx_copy.wait()
    x_exchange.wait()
    stream(u, urecv)
    for b in range(2):
        gx[b] = stream_out(b)
    for k in range(1, chunks):
        lines_here(u, colu, 0, k)
        span(colu, coly, k)
        to_rows(coly, gy, 1, k)
    levels_here(upad, 0)

    done, started = 0, 0
    for k in range(chunks):
        rows_here(coly, gy, 1, k)
        over_slabs(done, groups_ready(k), fluxes)
        done = groups_ready(k)
        while started < chunks and groups_needed(started) <= done:
            to_lines(fy, colf, 2, started)
            started += 1

    flux_exchange = exchange(fx, frecv, 1)
    flux_exchange.start()
    send_levels(fz, 1)

    columns = index.shape[1]
    third = columns // 3
    weight = jnp.zeros((1, columns), F32)
    for t in range(table.shape[0]):
        weight = weight + jnp.where(index[...] == t, table[t], 0.0)
    weight = jnp.broadcast_to(weight, (8, columns))
    cell = lax.broadcasted_iota(jnp.int32, (width, columns), 0)
    chosen = jnp.where(cell == source[...], 1.0, 0.0).astype(BF16)
    plane = lax.broadcasted_iota(jnp.int32, (columns, LANES), 0)
    slot = lax.broadcasted_iota(jnp.int32, (columns, LANES), 1)
    picks, weights = [], []
    for b in range(2):
        first = 2 * g if b == 0 else 1 - 4 * columns * g
        spread = jnp.where(
            jnp.logical_and(plane == 3 * slot + first, slot < third), 1.0, 0.0
        )
        picks.append(dot(chosen, spread.astype(BF16)).astype(BF16))
        weights.append(
            jnp.dot(weight, spread, precision=lax.Precision.HIGHEST, preferred_element_type=F32)
        )

    lines_here(fy, colf, 2, 0)
    span(colf, cold, 0)
    to_rows(cold, dy, 3, 0)
    flux_exchange.wait()
    stream(fx, frecv)
    for b in range(2):
        gx[b] = stream_out(b)
    for k in range(1, chunks):
        lines_here(fy, colf, 2, k)
        span(colf, cold, k)
        to_rows(cold, dy, 3, k)
    levels_here(fz, 1)
    over_slabs(0, group_count, add_rest)

    def blend(b, feed):
        high, low = feed
        fed = (dot(high, picks[b]) + dot(low, picks[b])).reshape(3, levels, rows, LANES)
        head = out[b, :, :, :, :LANES]
        out[b, :, :, :, :LANES] = head + weights[b][0:1] * (fed - head)

    inflow_copy = pltpu.make_async_remote_copy(
        src_ref=out.at[1], dst_ref=inflow, send_sem=isend, recv_sem=irecv,
        device_id={"grp": other}, device_id_type=MESH,
    )
    done = 0
    for k in range(chunks):
        rows_here(cold, dy, 3, k)
        ready = groups_ready(k)
        half = group_count // 2
        if done < half <= ready:
            over_slabs(done, half, add_span)
            done = half

            @pl.when(g == 1)
            def _():
                inflow_copy.start()
                inflow[...] = out[1]

        over_slabs(done, ready, add_span)
        done = ready

    @pl.when(g == 0)
    def _():
        inflow_copy.wait_recv()

    @pl.when(g == 1)
    def _():
        inflow_copy.wait_send()

    feed = split(inflow[...].reshape(3 * levels * rows, width))
    for b in range(2):
        blend(b, feed)
    for phase, src, dst in (
        (0, u.at[unit(0, 0)], colu.at[0, band(0)]),
        (1, coly.at[0, band(0)], gy.at[unit(0, 0)]),
        (2, fy.at[unit(0, 0)], colf.at[0, band(0)]),
        (3, cold.at[0, band(0)], dy.at[unit(0, 0)]),
    ):
        sent(src, dst, phase)


def per_device(pens, heights, velocity, source, index, table):
    _, _, levels, rows, width = velocity.shape
    line = rows * pens
    chunks = 2 * 3 * levels * (width // LANES) // pens
    wx = two_parts(stream_table(width))
    wy = two_parts(span_table(line, pens))
    flat = 3 * levels * rows
    whole = pltpu.VMEM(velocity.shape, F32)
    padded = pltpu.VMEM((2, 3, levels + 2, rows, width), F32)
    lines = pltpu.VMEM((chunks, line, LANES), F32)
    vmem = pl.BlockSpec(memory_space=pltpu.VMEM)
    dma = pltpu.SemaphoreType.DMA
    return pl.pallas_call(
        functools.partial(kernel, pens, heights),
        out_shape=jax.ShapeDtypeStruct(velocity.shape, F32),
        in_specs=[
            vmem, vmem, vmem, pl.BlockSpec(memory_space=pltpu.SMEM),
            pl.BlockSpec(memory_space=pl.ANY), pl.BlockSpec(memory_space=pl.ANY),
        ],
        out_specs=vmem,
        scratch_shapes=[
            pltpu.VMEM((2, 4 * width, 2 * width), BF16),
            pltpu.VMEM((2, line, line), BF16),
            padded, whole, whole, whole, whole, whole, padded, whole, whole, whole,
            lines, lines, lines, lines,
            pltpu.VMEM((flat, 4 * width), BF16),
            pltpu.VMEM((flat, 4 * width), BF16),
            pltpu.VMEM(velocity.shape[1:], F32),
            dma((4, chunks, pens)), dma((4, chunks, pens)),
            dma((2,)), dma((2,)), dma((2, 2)), dma((2, 2)), dma, dma, dma((3,)),
        ],
        compiler_params=pltpu.CompilerParams(
            collective_id=0, has_side_effects=True, vmem_limit_bytes=56 * 1024 * 1024
        ),
    )(velocity, source.reshape(1, -1), index.reshape(1, -1), table, jnp.asarray(wx), jnp.asarray(wy))


def solution(mesh):
    placed = P("grp", None, "gz", "pen", None)
    return jax.shard_map(
        functools.partial(per_device, mesh.shape["pen"], mesh.shape["gz"]),
        mesh=mesh,
        in_specs=(placed, P(), P(), P()),
        out_specs=placed,
        check_vma=False,
    )
```

time: 261 us -> 81.3 us (0.31); the launches traced: 258 us -> 81.2 us
  matrix products: 83.8 us -> 0 us
  Pallas kernels: 0 us -> 79.1 us
  local copies, waits for them, and re-layouts: 61.4 us -> 2.06 us
  waiting for transfers between devices: 40.1 us -> 0 us
  starting transfers between devices: 36.3 us -> 0 us
  other arithmetic: 22.3 us -> 0 us
  between operations: 14.2 us -> 0.01 us
    dot_general x4 -> x0, matrix products: 83.8 us -> none  [the longest x2 69.3 us: add_stream_terms(): return jnp.einsum('mczyl,jiml->jczyi', shards, operator, precision=HIGHEST)]
    pallas_call x0 -> x1, Pallas kernels: none -> 79.1 us  [per_device(): pl.pallas_call(functools.partial(kernel, pens, heights), out_shape=jax.Sh...]
    all_to_all x4 -> x0, waiting for transfers between devices: 37.5 us -> none  [the longest x1 19.1 us: per_device(): lax.all_to_all(fluxes[1], 'pen', split_axis=4, concat_axis=3, tiled=True)]
    unnamed x54 -> x1, local copies, waits for them, and re-layouts: 31 us -> 2.06 us
    all_to_all x4 -> x0, starting transfers between devices: 20.4 us -> none  [the longest x1 7.25 us: per_device(): lax.all_to_all(velocity, 'pen', split_axis=4, concat_axis=3, tiled=True)]
    ppermute x5 -> x0, starting transfers between devices: 15.7 us -> none  [the longest x2 11.9 us: with_halo(): lax.ppermute(tail, axis, [(i, (i + 1) % count) for i in range(ends)])]
    all_to_all x11 -> x0, local copies, waits for them, and re-layouts: 14.4 us -> none  [the longest x2 5.31 us: per_device(): lax.all_to_all(span_derivative(flux_columns), 'pen', split_axis=3, concat...]
    all_to_all x4 -> x0, other arithmetic: 11.1 us -> none  [the longest x1 3.66 us: per_device(): lax.all_to_all(fluxes[1], 'pen', split_axis=4, concat_axis=3, tiled=True)]
  transfers between devices with their start and end apart: 11 -> 0, of which waited for: 4 -> 0; matrix products, arithmetic and copies ran while one was open for 41% -> 0% of each run, Pallas kernels for 0% -> 0%
where the time goes in v1:
time: 81.3 us; the launch traced here: 81.2 us
  Pallas kernels  79.1 us (97%)
  local copies, waits for them, and re-layouts  2.06 us (3%)
    pallas_call x1, Pallas kernels, per_device(): pl.pallas_call(functools.partial(kernel, pens, heights), out_shape=jax.Sh...  79.1 us
    unnamed x1, local copies, waits for them, and re-layouts  2.06 us

profile of v1, /device:TPU:0, one launch (start us, length us, event | category | flops | bytes accessed | tf_op | source)
XLA Modules:
  0.0 81.2 jit_solution(18385468215307198320)
XLA Ops:
  0.0 79.1 %shard_map.64 = f32[2,3,2,64,256]{4,3,2,1,0:T(8,128)} custom-call(f32[2,3,2,64,256]{4,3,2,1,0:T(8,128)} %u.1, s32[1,192]{1,0:T(1,128)} %bitcast.2, s32[1,192]{1,0:T(1,128)} %bitcast.3, f32[16]{0:T(128)} %table.1, bf16[2,2,1024,512]{3,2,1,0:T(8,128)(2,1)} %constant.4.clone.wx_hbm, bf16[2,512,512]{2,1,0:T(8,128)(2,1)} %constant.5.clone.wy_hbm), custom_call_target="tpu_custom_call" | custom-call | tf_op jit(solution)/shard_map/pallas_call | solution.py:422
  79.1 2.1 %copy.8 = f32[2,3,2,64,256]{4,3,2,1,0:T(8,128)} copy(f32[2,3,2,64,256]{4,3,2,1,0:T(8,128)} %shard_map.64) | data formatting | bytes 1572864

commit v2 on v1

--- a/solution.py
+++ b/solution.py
@@ -74,7 +74,7 @@
 def kernel(
     pens, heights, u, source, index, table, wx_hbm, wy_hbm, out,
     wx, wy, upad, urecv, gx, gy, fx, fy, fz, frecv, acc, dy, colu, coly, colf, cold,
-    hi, lo, inflow, send, recv, esend, erecv, hsend, hrecv, isend, irecv, lsem,
+    hi, lo, inflow, fed, send, recv, esend, erecv, hsend, hrecv, isend, irecv, lsem,
 ):
     g = lax.axis_index("grp")
     me = lax.axis_index("pen")
@@ -86,13 +86,6 @@
     other = 1 - g
     below, above = s > 0, s < heights - 1
 
-    wx_copy = pltpu.make_async_copy(wx_hbm.at[:, g], wx, lsem.at[0])
-    wy_copy = pltpu.make_async_copy(wy_hbm, wy, lsem.at[1])
-    u_copy = pltpu.make_async_copy(u, upad.at[:, :, pl.ds(1, levels)], lsem.at[2])
-    wy_copy.start()
-    wx_copy.start()
-    u_copy.start()
-
     barrier = pltpu.get_barrier_semaphore()
 
     @pl.loop(1, pens)
@@ -111,6 +104,13 @@
     def _():
         pl.semaphore_signal(barrier, inc=1, device_id={"gz": s + 1}, device_id_type=MESH)
 
+    wx_copy = pltpu.make_async_copy(wx_hbm.at[:, g], wx, lsem.at[0])
+    wy_copy = pltpu.make_async_copy(wy_hbm, wy, lsem.at[1])
+    u_copy = pltpu.make_async_copy(u, upad.at[:, :, pl.ds(1, levels)], lsem.at[2])
+    u_copy.start()
+    wy_copy.start()
+    wx_copy.start()
+
     levels_near = below.astype(jnp.int32) + above.astype(jnp.int32)
     pl.semaphore_wait(barrier, pens + levels_near)
 
@@ -188,8 +188,8 @@
 
     def stream(mine, theirs):
         for b in range(2):
-            for at, field in ((b, mine), (b + 2, theirs)):
-                high, low = split(field[b].reshape(3 * levels * rows, width))
+            for at, field in ((b, mine(b)), (b + 2, theirs[b])):
+                high, low = split(field.reshape(3 * levels * rows, width))
                 hi[:, at * width : (at + 1) * width] = high
                 lo[:, at * width : (at + 1) * width] = low
 
@@ -251,7 +251,7 @@
             step(b, z, r, x)
 
     def fluxes(b, z, r, x):
-        speed = [u[b, c, z, r, x] for c in range(3)]
+        speed = [upad[b, c, z + 1, r, x] for c in range(3)]
         grad = [
             [gx[b, c, z, r, x] for c in range(3)],
             [gy[b, c, z, r, x] for c in range(3)],
@@ -278,7 +278,7 @@
         for c in range(3):
             rise = 0.5 * (fz[b, c, z + 2, r, x] - fz[b, c, z, r, x])
             total = acc[b, c, z, r, x] + gx[b, c, z, r, x] + rise
-            acc[b, c, z, r, x] = u[b, c, z, r, x] + TIMESTEP * total
+            acc[b, c, z, r, x] = upad[b, c, z + 1, r, x] + TIMESTEP * total
 
     def add_span(b, z, r, x):
         for c in range(3):
@@ -291,19 +291,21 @@
         return -(-((k + 1) * pens) // 3)
 
     x_exchange = exchange(u, urecv, 0)
-    x_exchange.start()
-    u_copy.wait()
-    for k in range(chunks):
+    for k in range(min(2, chunks)):
         to_lines(u, colu, 0, k)
         if k == 0:
-            send_levels(upad, 0)
+            x_exchange.start()
+    u_copy.wait()
+    send_levels(upad, 0)
     wy_copy.wait()
     lines_here(u, colu, 0, 0)
     span(colu, coly, 0)
     to_rows(coly, gy, 1, 0)
+    for k in range(2, chunks):
+        to_lines(u, colu, 0, k)
     wx_copy.wait()
     x_exchange.wait()
-    stream(u, urecv)
+    stream(lambda b: upad[b, :, 1 : levels + 1], urecv)
     for b in range(2):
         gx[b] = stream_out(b)
     for k in range(1, chunks):
@@ -350,7 +352,7 @@
     span(colf, cold, 0)
     to_rows(cold, dy, 3, 0)
     flux_exchange.wait()
-    stream(fx, frecv)
+    stream(lambda b: fx[b], frecv)
     for b in range(2):
         gx[b] = stream_out(b)
     for k in range(1, chunks):
@@ -360,21 +362,22 @@
     levels_here(fz, 1)
     over_slabs(0, group_count, add_rest)
 
-    def blend(b, feed):
-        high, low = feed
-        fed = (dot(high, picks[b]) + dot(low, picks[b])).reshape(3, levels, rows, LANES)
-        head = out[b, :, :, :, :LANES]
-        out[b, :, :, :, :LANES] = head + weights[b][0:1] * (fed - head)
+    def feed(b, parts):
+        both = dot(parts[0], picks[b]) + dot(parts[1], picks[b])
+        fed[b] = both.reshape(3, levels, rows, LANES)
+
+    def blend(b, z):
+        head = out[b, :, z, :, :LANES]
+        out[b, :, z, :, :LANES] = head + weights[b][0:1] * (fed[b, :, z] - head)
 
     inflow_copy = pltpu.make_async_remote_copy(
         src_ref=out.at[1], dst_ref=inflow, send_sem=isend, recv_sem=irecv,
         device_id={"grp": other}, device_id_type=MESH,
     )
-    done = 0
+    done, half = 0, group_count // 2
     for k in range(chunks):
         rows_here(cold, dy, 3, k)
         ready = groups_ready(k)
-        half = group_count // 2
         if done < half <= ready:
             over_slabs(done, half, add_span)
             done = half
@@ -384,20 +387,27 @@
                 inflow_copy.start()
                 inflow[...] = out[1]
 
-        over_slabs(done, ready, add_span)
-        done = ready
-
-    @pl.when(g == 0)
-    def _():
-        inflow_copy.wait_recv()
-
-    @pl.when(g == 1)
-    def _():
-        inflow_copy.wait_send()
-
-    feed = split(inflow[...].reshape(3 * levels * rows, width))
-    for b in range(2):
-        blend(b, feed)
+            over_slabs(done, ready, add_span)
+            done = ready
+
+            @pl.when(g == 0)
+            def _():
+                inflow_copy.wait_recv()
+
+            @pl.when(g == 1)
+            def _():
+                inflow_copy.wait_send()
+
+            parts = split(inflow[...].reshape(3 * levels * rows, width))
+            for b in range(2):
+                feed(b, parts)
+            for z in range(levels):
+                blend(1, z)
+        elif done < ready:
+            over_slabs(done, ready, add_span)
+            done = ready
+    for z in range(levels):
+        blend(0, z)
     for phase, src, dst in (
         (0, u.at[unit(0, 0)], colu.at[0, band(0)]),
         (1, coly.at[0, band(0)], gy.at[unit(0, 0)]),
@@ -421,9 +431,9 @@
     dma = pltpu.SemaphoreType.DMA
     return pl.pallas_call(
         functools.partial(kernel, pens, heights),
-        out_shape=jax.ShapeDtypeStruct(velocity.shape, F32),
+        out_shape=pltpu.VMEM(velocity.shape, F32),
         in_specs=[
-            vmem, vmem, vmem, pl.BlockSpec(memory_space=pltpu.SMEM),
+            pl.BlockSpec(memory_space=pl.ANY), vmem, vmem, pl.BlockSpec(memory_space=pltpu.SMEM),
             pl.BlockSpec(memory_space=pl.ANY), pl.BlockSpec(memory_space=pl.ANY),
         ],
         out_specs=vmem,
@@ -435,6 +445,7 @@
             pltpu.VMEM((flat, 4 * width), BF16),
             pltpu.VMEM((flat, 4 * width), BF16),
             pltpu.VMEM(velocity.shape[1:], F32),
+            pltpu.VMEM((2, 3, levels, rows, LANES), F32),
             dma((4, chunks, pens)), dma((4, chunks, pens)),
             dma((2,)), dma((2,)), dma((2, 2)), dma((2, 2)), dma, dma, dma((3,)),
         ],

time: 81.3 us -> 77.8 us (0.957)
  Pallas kernels: 79.1 us -> 76.8 us
  local copies, waits for them, and re-layouts: 2.06 us -> 0.88 us
    pallas_call x1, Pallas kernels: 79.1 us -> 76.8 us  [per_device(): pl.pallas_call(functools.partial(kernel, pens, heights), out_shape=pltpu....]
    unnamed x1, local copies, waits for them, and re-layouts: 2.06 us -> 0.88 us
where the time goes in v2:
time: 77.8 us; the launch traced here: 77.6 us
  Pallas kernels  76.8 us (99%)
  local copies, waits for them, and re-layouts  0.88 us (1%)
    pallas_call x1, Pallas kernels, per_device(): pl.pallas_call(functools.partial(kernel, pens, heights), out_shape=pltpu....  76.8 us

profile of v2, /device:TPU:0, one launch (start us, length us, event | category | flops | bytes accessed | tf_op | source)
XLA Modules:
  0.0 77.6 jit_solution(5861647249617352425)
XLA Ops:
  0.0 76.8 %shard_map.64 = f32[2,3,2,64,256]{4,3,2,1,0:T(8,128)S(1)} custom-call(f32[2,3,2,64,256]{4,3,2,1,0:T(8,128)} %u.1, s32[1,192]{1,0:T(1,128)} %bitcast.2, s32[1,192]{1,0:T(1,128)} %bitcast.3, f32[16]{0:T(128)} %table.1, bf16[2,2,1024,512]{3,2,1,0:T(8,128)(2,1)} %constant.4.clone.wx_hbm, bf16[2,512,512]{2,1,0:T(8,128)(2,1)} %constant.5.clone.wy_hbm), custom_call_target="tpu_custom_call" | custom-call | tf_op jit(solution)/shard_map/pallas_call | solution.py:432
  76.8 0.9 %copy.8 = f32[2,3,2,64,256]{4,3,2,1,0:T(8,128)} copy(f32[2,3,2,64,256]{4,3,2,1,0:T(8,128)S(1)} %shard_map.64) | data formatting | bytes 1572864

commit v3 on v2

--- a/solution.py
+++ b/solution.py
@@ -299,19 +299,20 @@
     send_levels(upad, 0)
     wy_copy.wait()
     lines_here(u, colu, 0, 0)
+    for k in range(2, chunks):
+        to_lines(u, colu, 0, k)
     span(colu, coly, 0)
     to_rows(coly, gy, 1, 0)
-    for k in range(2, chunks):
-        to_lines(u, colu, 0, k)
-    wx_copy.wait()
-    x_exchange.wait()
-    stream(lambda b: upad[b, :, 1 : levels + 1], urecv)
-    for b in range(2):
-        gx[b] = stream_out(b)
     for k in range(1, chunks):
         lines_here(u, colu, 0, k)
         span(colu, coly, k)
         to_rows(coly, gy, 1, k)
+        if k == 1:
+            wx_copy.wait()
+            x_exchange.wait()
+            stream(lambda b: upad[b, :, 1 : levels + 1], urecv)
+            for b in range(2):
+                gx[b] = stream_out(b)
     levels_here(upad, 0)
 
     done, started = 0, 0

time: 77.8 us -> 77.7 us (level)
  no operation moved by 1% of the time
where the time goes in v3:
time: 77.7 us; the launch traced here: 77.5 us
  Pallas kernels  76.6 us (99%)
  local copies, waits for them, and re-layouts  0.88 us (1%)
    pallas_call x1, Pallas kernels, per_device(): pl.pallas_call(functools.partial(kernel, pens, heights), out_shape=pltpu....  76.6 us

profile of v3, /device:TPU:0, one launch (start us, length us, event | category | flops | bytes accessed | tf_op | source)
XLA Modules:
  0.0 77.5 jit_solution(17406521774904403247)
XLA Ops:
  0.0 76.6 %shard_map.64 = f32[2,3,2,64,256]{4,3,2,1,0:T(8,128)S(1)} custom-call(f32[2,3,2,64,256]{4,3,2,1,0:T(8,128)} %u.1, s32[1,192]{1,0:T(1,128)} %bitcast.2, s32[1,192]{1,0:T(1,128)} %bitcast.3, f32[16]{0:T(128)} %table.1, bf16[2,2,1024,512]{3,2,1,0:T(8,128)(2,1)} %constant.4.clone.wx_hbm, bf16[2,512,512]{2,1,0:T(8,128)(2,1)} %constant.5.clone.wy_hbm), custom_call_target="tpu_custom_call" | custom-call | tf_op jit(solution)/shard_map/pallas_call | solution.py:433
  76.6 0.9 %copy.8 = f32[2,3,2,64,256]{4,3,2,1,0:T(8,128)} copy(f32[2,3,2,64,256]{4,3,2,1,0:T(8,128)S(1)} %shard_map.64) | data formatting | bytes 1572864
